TPU v7x, 32 devices: a whole 2x2x4 slice. The times are simulated.
32 devices in a mesh: row: 8 (over z, y), col: 4 (over x, core).
Axes of the slice: x: 2, y: 2, z: 4, core: 2. Of those that a mesh axis runs over, the one named last changes fastest.
Arguments:
- right_side: float32 [4, 64, 6144], P(None, 'row'), may hold values from -6 to 6
- factor: bfloat16 [4, 64, 128, 4096], P(None, 'row', 'col'), may hold values from -0.0625 to 0.0625
- diagonal_block_inverse: bfloat16 [4, 64, 4096], P(None, 'row'), may hold values from -0.5 to 0.5
- pattern: int32 [4, 64, 128], P(None, 'row', 'col'), may hold values from -1 to 191, as said below
Outputs:
- solution: bfloat16 [4, 64, 6144], P(None, 'row')
Inputs may be any that keep to these rules, and one draw needn't show every extreme that they name: `pattern`: level 0 is all -1; at level l an entry is -1 or names a supernode of an earlier level, below l * 64.
All inputs are finite; a program needn't handle non-finite values.
Results may differ from a plain program's by a relative error of at most 0.0055.
Values may be sent and summed in bfloat16 or wider, within the bound.
A program may use at most 128 MiB of HBM per device.

v0:
```python
import jax
import jax.numpy as jnp
from jax import lax
from jax.sharding import PartitionSpec as P

B = 64
R = 96


def per_device(right_side, factor, diagonal_block_inverse, pattern):
    levels = right_side.shape[0]
    sn_dev = right_side.shape[1]
    slot_count = factor.shape[2]
    row_count = lax.axis_size("row")
    sn_lev = sn_dev * row_count
    panel_blocks = jnp.zeros((levels * sn_lev, B * R), jnp.bfloat16)
    for level in range(levels):
        present_level = right_side[level].reshape(sn_dev, B, R)
        inverse_block = diagonal_block_inverse[level].reshape(sn_dev, B, B)
        if level > 0:
            sources = pattern[level]
            active = sources >= 0
            clipped = jnp.maximum(sources, 0).reshape(-1)
            picked = jnp.take(panel_blocks, clipped, axis=0).reshape(sn_dev, slot_count, B * R)
            picked = jnp.where(active[:, :, None], picked, jnp.zeros_like(picked))
            picked = picked.reshape(sn_dev, slot_count, B, R)
            blocks = factor[level].reshape(sn_dev, slot_count, B, B)
            partial_value = jnp.einsum(
                "skab,skbr->sar", blocks, picked, preferred_element_type=jnp.float32
            )
        if level > 0:
            summed_products = lax.psum(partial_value, "col")
            reduced_rows = (present_level - summed_products).astype(jnp.bfloat16)
        else:
            reduced_rows = present_level.astype(jnp.bfloat16)
        solved_rows = jnp.einsum(
            "xuc,xcg->xug", inverse_block, reduced_rows, preferred_element_type=jnp.float32
        ).astype(jnp.bfloat16)
        complete = lax.all_gather(solved_rows, "row", axis=0, tiled=True)
        panel_blocks = panel_blocks.at[level * sn_lev : (level + 1) * sn_lev].set(
            complete.reshape(sn_lev, B * R)
        )
    arranged = panel_blocks.reshape(levels, row_count, sn_dev, B * R)
    return lax.dynamic_index_in_dim(arranged, lax.axis_index("row"), 1, False)


def solution(mesh):
    return jax.shard_map(
        per_device,
        mesh=mesh,
        in_specs=(
            P(None, "row", None),
            P(None, "row", "col", None),
            P(None, "row", None),
            P(None, "row", "col"),
        ),
        out_specs=P(None, "row", None),
        check_vma=False,
    )
```

profile of v0, /device:TPU:0, one launch (start us, length us, event | category | flops | bytes accessed | tf_op | source)
XLA Modules:
  0.0 352.1 jit_solution(10764887164622841135)
XLA Ops:
  7.4 1.3 compare_bitcast_fusion
  8.7 1.6 fusion.29
  11.7 34.6 %all_gather.12 = bf16[64,64,96]{2,1,0:T(8,128)(2,1)S(1)} all-gather(bf16[8,64,96]{2,1,0:T(8,128)(2,1)S(1)} %convolution_convert_fusion.3), channel_id=1, replica_groups=mesh['row'=8,'col'=4] {'row'}, dimensions={0}, use_global_device_ids=true | all-gather | bytes 884736 | tf_op jit(solution)/shard_map/all_gather | solution.py:39
  46.3 2.3 reshape.164
  48.6 1.4 scatter.14
  50.0 4.1 %gather_fusion = bf16[256,6144]{1,0:T(8,128)(2,1)} fusion(bf16[256,6144]{1,0:T(8,128)(2,1)S(1)} %scatter.14, s32[1024]{0:T(1024)S(1)} %pad_clamp_fusion.2), kind=kCustom, calls=%fused_computation.clone | custom fusion | bytes 6292480 | tf_op jit(solution)/shard_map/jit(_take)/gather | solution.py:24
  54.1 3.9 %broadcast_select_fusion.2 = bf16[256,6144]{1,0:T(8,128)(2,1)} fusion(bf16[256,6144]{1,0:T(8,128)(2,1)} %gather_fusion, pred[256]{0:T(512)(128)(4,1)S(1)} %compare_and_fusion.2), kind=kLoop, calls=%fused_computation.14 | loop fusion | flops 1572864 | bytes 6291712 | tf_op jit(solution)/shard_map/jit(_take)/select_n | solution.py:24
  58.1 7.8 %reshape.165 = bf16[8,32,64,96]{3,2,1,0:T(8,128)(2,1)} reshape(bf16[256,6144]{1,0:T(8,128)(2,1)} %broadcast_select_fusion.2) | data formatting | bytes 6291456 | tf_op jit(solution)/shard_map/reshape | solution.py:24
  65.8 5.7 %fusion.27 = (bf16[1,8,32,4096]{3,2,1,0:T(8,128)(2,1)}, bf16[1,8,32,4096]{3,2,1,0:T(8,128)(2,1)}, bf16[1,8,32,4096]{3,2,1,0:T(8,128)(2,1)}) fusion(bf16[4,8,32,4096]{3,2,1,0:T(8,128)(2,1)} %param.15), kind=kLoop, calls=%fused_computation.54 | loop fusion | bytes 12582912 | tf_op jit(solution)/shard_map/slice | solution.py:27
  71.5 6.9 %reshape_squeeze.33 = bf16[8,32,64,64]{3,2,1,0:T(8,128)(2,1)} reshape(bf16[1,8,32,4096]{3,2,1,0:T(8,128)(2,1)} %get-tuple-element.55) | data formatting | bytes 4194304 | tf_op jit(solution)/shard_map/reshape;squeeze | solution.py:27
  78.4 5.3 %fusion.12 = f32[8,64,96]{2,1,0:T(8,128)} fusion(bf16[8,32,64,64]{3,2,1,0:T(8,128)(2,1)} %reshape_squeeze.33, bf16[8,32,64,96]{3,2,1,0:T(8,128)(2,1)} %reshape.165, pred[8,32]{1,0:T(8,128)(4,1)S(1)} %get-tuple-element.65), kind=kOutput, calls=%fused_computation.18 | convolution fusion | flops 202899456 | bytes 5439744 | tf_op jit(solution)/shard_map/skab,skbr->sar/dot_general | solution.py:28
  83.7 1.9 fusion.28
  88.1 6.9 %reshape_squeeze.36 = bf16[8,32,64,64]{3,2,1,0:T(8,128)(2,1)} reshape(bf16[1,8,32,4096]{3,2,1,0:T(8,128)(2,1)} %get-tuple-element.56) | data formatting | bytes 4194304 | tf_op jit(solution)/shard_map/reshape;squeeze | solution.py:27
  96.3 6.9 %reshape_squeeze.39 = bf16[8,32,64,64]{3,2,1,0:T(8,128)(2,1)} reshape(bf16[1,8,32,4096]{3,2,1,0:T(8,128)(2,1)} %get-tuple-element.54) | data formatting | bytes 4194304 | tf_op jit(solution)/shard_map/reshape;squeeze | solution.py:27
  103.2 13.5 %all-reduce.5.cloned.1.call-done = f32[8,64,96]{2,1,0:T(8,128)} async-done(((f32[8,64,96]{2,1,0:T(8,128)}), f32[8,64,96]{2,1,0:T(8,128)}) %all-reduce.5.cloned.1.call-update) | async-done | bytes 196624 | tf_op jit(solution)/shard_map/psum | solution.py:32
  116.7 1.3 fusion.21
  118.0 35.2 %all_gather.13 = bf16[64,64,96]{2,1,0:T(8,128)(2,1)} all-gather(bf16[8,64,96]{2,1,0:T(8,128)(2,1)S(1)} %fusion.21), channel_id=1, replica_groups=mesh['row'=8,'col'=4] {'row'}, dimensions={0}, use_global_device_ids=true | all-gather | bytes 884736 | tf_op jit(solution)/shard_map/all_gather | solution.py:39
  153.2 3.2 reshape.166
  157.6 4.1 %gather_fusion.1 = bf16[256,6144]{1,0:T(8,128)(2,1)} fusion(bf16[256,6144]{1,0:T(8,128)(2,1)S(1)} %constant_dynamic-update-slice_fusion.2, s32[1024]{0:T(1024)S(1)} %pad_clamp_fusion.1), kind=kCustom, calls=%fused_computation.1.clone | custom fusion | bytes 6292480 | tf_op jit(solution)/shard_map/jit(_take)/gather | solution.py:24
  161.7 3.9 %broadcast_select_fusion.1 = bf16[256,6144]{1,0:T(8,128)(2,1)} fusion(bf16[256,6144]{1,0:T(8,128)(2,1)} %gather_fusion.1, pred[256]{0:T(512)(128)(4,1)S(1)} %copy-done.1), kind=kLoop, calls=%fused_computation.13 | loop fusion | flops 1572864 | bytes 6291712 | tf_op jit(solution)/shard_map/jit(_take)/select_n | solution.py:24
  165.6 7.8 %reshape.167 = bf16[8,32,64,96]{3,2,1,0:T(8,128)(2,1)} reshape(bf16[256,6144]{1,0:T(8,128)(2,1)} %broadcast_select_fusion.1) | data formatting | bytes 6291456 | tf_op jit(solution)/shard_map/reshape | solution.py:24
  173.3 5.3 %fusion.15 = f32[8,64,96]{2,1,0:T(8,128)} fusion(bf16[8,32,64,64]{3,2,1,0:T(8,128)(2,1)} %reshape_squeeze.36, bf16[8,32,64,96]{3,2,1,0:T(8,128)(2,1)} %reshape.167, pred[8,32]{1,0:T(8,128)(4,1)S(1)} %copy-done.3), kind=kOutput, calls=%fused_computation.19 | convolution fusion | flops 202899456 | bytes 5439744 | tf_op jit(solution)/shard_map/skab,skbr->sar/dot_general | solution.py:28
  178.7 31.8 %all-reduce.7.cloned.1.call-done = f32[8,64,96]{2,1,0:T(8,128)} async-done(((f32[8,64,96]{2,1,0:T(8,128)}), f32[8,64,96]{2,1,0:T(8,128)}) %all-reduce.7.cloned.1.call-update) | async-done | bytes 196624 | tf_op jit(solution)/shard_map/psum | solution.py:32
  211.7 34.9 %all_gather.14 = bf16[64,64,96]{2,1,0:T(8,128)(2,1)} all-gather(bf16[8,64,96]{2,1,0:T(8,128)(2,1)S(1)} %fusion.22), channel_id=1, replica_groups=mesh['row'=8,'col'=4] {'row'}, dimensions={0}, use_global_device_ids=true | all-gather | bytes 884736 | tf_op jit(solution)/shard_map/all_gather | solution.py:39
  246.6 3.2 reshape.168
  251.0 4.2 %gather_fusion.2 = bf16[256,6144]{1,0:T(8,128)(2,1)} fusion(bf16[256,6144]{1,0:T(8,128)(2,1)S(1)} %constant_dynamic-update-slice_fusion.1, s32[1024]{0:T(1024)S(1)} %pad_clamp_fusion), kind=kCustom, calls=%fused_computation.2.clone | custom fusion | bytes 6292480 | tf_op jit(solution)/shard_map/jit(_take)/gather | solution.py:24
  255.2 4.0 %broadcast_select_fusion = bf16[256,6144]{1,0:T(8,128)(2,1)} fusion(bf16[256,6144]{1,0:T(8,128)(2,1)} %gather_fusion.2, pred[256]{0:T(512)(128)(4,1)S(1)} %get-tuple-element.70), kind=kLoop, calls=%fused_computation.12 | loop fusion | flops 1572864 | bytes 6291712 | tf_op jit(solution)/shard_map/jit(_take)/select_n | solution.py:24
  259.2 7.8 %reshape.169 = bf16[8,32,64,96]{3,2,1,0:T(8,128)(2,1)} reshape(bf16[256,6144]{1,0:T(8,128)(2,1)} %broadcast_select_fusion) | data formatting | bytes 6291456 | tf_op jit(solution)/shard_map/reshape | solution.py:24
  267.0 5.3 %fusion.18 = f32[8,64,96]{2,1,0:T(8,128)} fusion(bf16[8,32,64,64]{3,2,1,0:T(8,128)(2,1)} %reshape_squeeze.39, bf16[8,32,64,96]{3,2,1,0:T(8,128)(2,1)} %reshape.169, pred[8,32]{1,0:T(8,128)(4,1)S(1)} %copy-done.2), kind=kOutput, calls=%fused_computation.20 | convolution fusion | flops 202899456 | bytes 5439744 | tf_op jit(solution)/shard_map/skab,skbr->sar/dot_general | solution.py:28
  273.6 30.7 %all-reduce.9.cloned.1.call-done = f32[8,64,96]{2,1,0:T(8,128)} async-done(((f32[8,64,96]{2,1,0:T(8,128)}), f32[8,64,96]{2,1,0:T(8,128)}) %all-reduce.9.cloned.1.call-update) | async-done | bytes 196624 | tf_op jit(solution)/shard_map/psum | solution.py:32
  305.4 35.0 %all_gather.15 = bf16[64,64,96]{2,1,0:T(8,128)(2,1)} all-gather(bf16[8,64,96]{2,1,0:T(8,128)(2,1)S(1)} %fusion.23), channel_id=1, replica_groups=mesh['row'=8,'col'=4] {'row'}, dimensions={0}, use_global_device_ids=true | all-gather | bytes 884736 | tf_op jit(solution)/shard_map/all_gather | solution.py:39
  340.4 3.2 reshape.170
  (42 shorter events, 13.9 us)
Async XLA Ops:
  6.5 110.2 %all-reduce.5.cloned.1.call-start = ((), (), s32[]{:S(2)}) async-start(), calls=%async_computation | async-start | bytes 524288 | tf_op jit(solution)/shard_map/psum | solution.py:32
  83.7 126.8 %all-reduce.7.cloned.1.call-start = ((), (), s32[]{:S(2)}) async-start(), calls=%async_computation.1 | async-start | bytes 524288 | tf_op jit(solution)/shard_map/psum | solution.py:32
  157.6 4.1 %copy-start.1 = (pred[256]{0:T(512)(128)(4,1)S(1)}, pred[256]{0:T(512)(128)(4,1)}, u32[]{:S(2)}) copy-start(pred[256]{0:T(512)(128)(4,1)} %get-tuple-element.71) | copy-start | bytes 772
  165.6 7.8 %copy-start.3 = (pred[8,32]{1,0:T(8,128)(4,1)S(1)}, pred[8,32]{1,0:T(8,128)(4,1)}, u32[]{:S(2)}) copy-start(pred[8,32]{1,0:T(8,128)(4,1)} %get-tuple-element.66) | copy-start | bytes 772
  178.6 125.6 %all-reduce.9.cloned.1.call-start = ((), (), s32[]{:S(2)}) async-start(), calls=%async_computation.2 | async-start | bytes 524288 | tf_op jit(solution)/shard_map/psum | solution.py:32
  259.2 7.8 %copy-start.2 = (pred[8,32]{1,0:T(8,128)(4,1)S(1)}, pred[8,32]{1,0:T(8,128)(4,1)}, u32[]{:S(2)}) copy-start(pred[8,32]{1,0:T(8,128)(4,1)} %get-tuple-element.64) | copy-start | bytes 772
  267.0 5.3 %copy-start = (bf16[1,8,4096]{2,1,0:T(8,128)(2,1)S(1)}, bf16[1,8,4096]{2,1,0:T(8,128)(2,1)}, u32[]{:S(2)}) copy-start(bf16[1,8,4096]{2,1,0:T(8,128)(2,1)} %get-tuple-element.60) | copy-start | bytes 196612
Sparse Core Ops, SparseCore 0:
  83.8 32.8 all-reduce.4
  178.8 31.7 all-reduce.6
  272.4 31.7 all-reduce.8
where the time goes:
time: 354 us; the launch traced here: 352 us
  blocking collectives  140 us (40%)
  local copies, waits for them, and re-layouts  89 us (25%)
  waiting for transfers between devices  76.1 us (21%)
  matrix products  19.5 us (6%)
  other arithmetic  14.4 us (4%)
  between operations  13.3 us (4%)
    all_gather x4, blocking collectives, per_device(): complete = lax.all_gather(solved_rows, 'row', axis=0, tiled=True)  140 us
    psum x3, waiting for transfers between devices, per_device(): summed_products = lax.psum(partial_value, 'col')  76.1 us
    reshape x3, local copies, waits for them, and re-layouts, per_device(): jnp.take(panel_blocks, clipped, axis=0).reshape(sn_dev, slot_count, B * R)  23.4 us
    another operation x3, local copies, waits for them, and re-layouts, per_device(): blocks = factor[level].reshape(sn_dev, slot_count, B, B)  20.7 us
    dot_general x3, matrix products, per_device(): jnp.einsum('skab,skbr->sar', blocks, picked, preferred_element_type=jnp.f...  15.8 us
    gather x3, local copies, waits for them, and re-layouts, per_device(): jnp.take(panel_blocks, clipped, axis=0).reshape(sn_dev, slot_count, B * R)  12.3 us
    another operation x4, local copies, waits for them, and re-layouts  12 us
    select_n x6, other arithmetic, per_device(): jnp.take(panel_blocks, clipped, axis=0).reshape(sn_dev, slot_count, B * R)  11.8 us
  transfers between devices with their start and end apart: 3, of which 3 were waited for; matrix products, arithmetic and copies ran while one was open for 6% of the time, Pallas kernels for 0%

commit v1 on v0

v1 whole, which is shorter than its diff:
```python
import functools

import jax
import jax.numpy as jnp
from jax import lax
from jax.experimental import pallas as pl
from jax.experimental.pallas import tpu as pltpu
from jax.sharding import PartitionSpec as P

B = 64
R = 96
LANES = 128
PACK = 48
MESH = pl.DeviceIdType.MESH


def pack(value):
    tail = value[PACK:, :R]
    third = B - PACK
    side = jnp.concatenate([tail[:, 32 * j : 32 * j + 32] for j in range(PACK // third)], axis=0)
    return jnp.concatenate([value[:PACK, :R], side], axis=1)


def unpack_tail(packed):
    third = B - PACK
    parts = [packed[third * j : third * (j + 1), R:] for j in range(PACK // third)]
    return jnp.concatenate(parts, axis=1)


def kernel(
    sizes, pattern_ref, right_ref, inverse_ref, factor_ref, out_ref,
    raw, ready, turn, panels, psend, mine, precv, land, last,
    fsem, red_send, red_recv, z_send, y_send, x_send, c_send,
    z_recv, y_recv, x_recv, c_recv, l_send, l_recv,
):
    levels, sn_dev, slots, Z, Y, X = sizes
    col_count = 2 * X
    row_count = Z * Y
    own = sn_dev // col_count
    sn_lev = sn_dev * row_count
    empty = (levels - 1) * sn_lev
    row = lax.axis_index("row")
    col = lax.axis_index("col")
    z, y = row // Y, row % Y
    x, core = col // 2, col % 2

    loads = [
        pltpu.make_async_copy(factor_ref.at[l + 1], raw.at[l], fsem.at[l]) for l in range(levels - 1)
    ]
    for load in loads:
        load.start()

    zs = [(z + d) % Z for d in range(1, Z)]
    ys = [(y + d) % Y for d in range(1, Y)]
    xs = [(x + d) % X for d in range(1, X)]
    cols = [(col + d) % col_count for d in range(1, col_count)]

    def at(r, c):
        return {"row": r, "col": c}

    barrier = pltpu.get_barrier_semaphore()
    for t in zs:
        pl.semaphore_signal(barrier, inc=1, device_id=at(t * Y + y, col), device_id_type=MESH)
    for t in ys:
        pl.semaphore_signal(barrier, inc=1, device_id=at(z * Y + t, col), device_id_type=MESH)
    for t in cols:
        pl.semaphore_signal(barrier, inc=1, device_id=at(row, t), device_id_type=MESH)

    def remote(src, dst, send, recv, device):
        return pltpu.make_async_remote_copy(
            src_ref=src, dst_ref=dst, send_sem=send, recv_sem=recv,
            device_id=device, device_id_type=MESH,
        )

    def solve(level, summed):
        for u in range(own):
            value = right_ref[level, u]
            if summed is not None:
                value = value - summed[u]
            solved = jnp.dot(
                inverse_ref[level, u], value.astype(jnp.bfloat16), preferred_element_type=jnp.float32
            )
            mine[level, u * PACK : (u + 1) * PACK, :] = pack(solved).astype(jnp.bfloat16)

    def prepare(level):
        loads[level - 1].wait()
        low = lax.broadcasted_iota(jnp.int32, (B // 2, LANES), 1) < B

        def body(i, carry):
            for a in range(B // 2):
                turn[:, a, :] = raw[level - 1, i, :, a * LANES : (a + 1) * LANES].astype(jnp.float32)
            for q in range(slots // 2):
                first, second = turn[2 * q], turn[2 * q + 1]
                lanes = slice(q * LANES, (q + 1) * LANES)
                ready[level - 1, i, : B // 2, lanes] = jnp.where(
                    low, first, pltpu.roll(second, B, 1)
                ).astype(jnp.bfloat16)
                ready[level - 1, i, B // 2 :, lanes] = jnp.where(
                    low, pltpu.roll(first, B, 1), second
                ).astype(jnp.bfloat16)
            return carry

        lax.fori_loop(0, sn_dev, body, 0)

    def products(level):
        def body(n, carry):
            target = (col + 1 + n // own) % col_count
            u = n % own
            i = target * own + u
            total = jnp.zeros((B, LANES), jnp.float32)
            for q in range(slots // 4):
                picked = []
                for k in range(4 * q, 4 * q + 4):
                    source = pattern_ref[level, i, k]
                    picked.append(panels[jnp.where(source < 0, empty, source)])
                total += jnp.dot(
                    ready[level - 1, i, :, 4 * B * q : 4 * B * (q + 1)],
                    jnp.concatenate(picked, axis=0),
                    preferred_element_type=jnp.float32,
                )
            psend[target, pl.ds(pl.multiple_of(u * PACK, PACK), PACK), :] = pack(total)
            return carry

        copies = []
        for d in range(1, col_count):
            lax.fori_loop((d - 1) * own, d * own, body, 0)
            t = cols[d - 1]
            copy = remote(
                psend.at[t], precv[level - 1].at[col],
                red_send.at[t], red_recv.at[level - 1, col], at(row, t),
            )
            copy.start()
            copies.append(copy)
        lax.fori_loop((col_count - 1) * own, col_count * own, body, 0)
        summed = psend[col]
        for t in cols:
            remote(
                psend.at[t], precv[level - 1].at[t],
                red_send.at[t], red_recv.at[level - 1, t], at(row, t),
            ).wait_recv()
            summed += precv[level - 1][t]
        for copy in copies:
            copy.wait_send()
        values = []
        for u in range(own):
            packed = summed[u * PACK : (u + 1) * PACK]
            values.append(jnp.concatenate([packed[:, :R], unpack_tail(packed)], axis=0))
        return values

    def spread(peers, where, region, land_level, send, recv, index):
        copies = []
        for t in peers:
            copy = remote(region(index), region(index), send.at[t], recv.at[index], where(t))
            copy.start()
            copies.append(copy)
        return copies

    def collect(peers, where, region, send, recv):
        for t in peers:
            remote(region(t), region(t), send.at[t], recv.at[t], where(t)).wait_recv()

    def gather(level, beside):
        here = land[level]
        own_copy = pltpu.make_async_copy(mine.at[level], here.at[z, y, x, core], fsem.at[levels - 1])
        own_copy.start()
        own_copy.wait()

        def z_region(t):
            return here.at[t, y, x, core]

        def z_where(t):
            return at(t * Y + y, col)

        def y_where(t):
            return at(z * Y + t, col)

        def x_where(t):
            return at(row, t * 2 + core)

        zc = spread(zs, z_where, z_region, here, z_send, z_recv.at[level], z)
        beside()
        collect(zs, z_where, z_region, z_send, z_recv.at[level])

        def along(y_region, x_region, y_first):
            def do_y():
                cs = spread(ys, y_where, y_region, here, y_send, y_recv.at[level], y)
                collect(ys, y_where, y_region, y_send, y_recv.at[level])
                return cs

            def do_x():
                cs = spread(xs, x_where, x_region, here, x_send, x_recv.at[level], x)
                collect(xs, x_where, x_region, x_send, x_recv.at[level])
                return cs

            cs = do_y() + do_x() if y_first else do_x() + do_y()
            for copy in cs:
                copy.wait_send()

        @pl.when(core == 0)
        def _():
            along(lambda t: here.at[:, t, x, core], lambda t: here.at[:, :, t, core], True)

        @pl.when(core == 1)
        def _():
            along(lambda t: here.at[:, t, :, core], lambda t: here.at[:, y, t, core], False)

        for copy in zc:
            copy.wait_send()
        sibling = remote(
            here.at[:, :, :, core], here.at[:, :, :, core],
            c_send.at[0], c_recv.at[level, core], at(row, x * 2 + 1 - core),
        )
        sibling.start()
        remote(
            here.at[:, :, :, 1 - core], here.at[:, :, :, 1 - core],
            c_send.at[0], c_recv.at[level, 1 - core], at(row, x * 2 + 1 - core),
        ).wait_recv()
        sibling.wait_send()

        def body(n, carry):
            zz = n // (Y * X)
            yy = (n // X) % Y
            xx = n % X
            base = level * sn_lev + n * (2 * own)
            for c in range(2):
                for u in range(own):
                    packed = here[zz, yy, xx, c, u * PACK : (u + 1) * PACK, :]
                    g = base + c * own + u
                    panels[g, :PACK, :] = packed
                    panels[g, PACK:, :R] = unpack_tail(packed)
            return carry

        lax.fori_loop(0, Z * Y * X, body, 0)

    panels[empty] = jnp.zeros((B, LANES), jnp.bfloat16)
    solve(0, None)
    pl.semaphore_wait(barrier, Z - 1 + Y - 1 + col_count - 1)
    for level in range(levels):
        if level > 0:
            solve(level, products(level))
        if level < levels - 1:
            gather(level, functools.partial(prepare, level + 1))
            for i in range(sn_dev):
                out_ref[level, i] = panels[level * sn_lev + row * sn_dev + i, :, :R]

    top = levels - 1
    copies = []
    for t in cols:
        copy = remote(mine.at[top], last.at[col], l_send.at[t], l_recv.at[col], at(row, t))
        copy.start()
        copies.append(copy)
    last[col] = mine[top]
    for t in cols:
        remote(mine.at[top], last.at[t], l_send.at[t], l_recv.at[t], at(row, t)).wait_recv()
    for copy in copies:
        copy.wait_send()
    for c in range(col_count):
        for u in range(own):
            packed = last[c, u * PACK : (u + 1) * PACK, :]
            out_ref[top, c * own + u, :PACK, :] = packed[:, :R]
            out_ref[top, c * own + u, PACK:, :] = unpack_tail(packed)


def per_device(right_side, factor, diagonal_block_inverse, pattern):
    levels, sn_dev, _ = right_side.shape
    slots = factor.shape[2]
    row_count = lax.axis_size("row")
    col_count = lax.axis_size("col")
    Y = 1
    while 8 * Y * Y <= row_count:
        Y *= 2
    Z = row_count // Y
    X = col_count // 2
    own = sn_dev // col_count
    sn_lev = sn_dev * row_count
    first = lax.axis_index("col") * own
    right = lax.dynamic_slice_in_dim(right_side, first, own, 1)
    right = right.reshape(levels, own, B // 2, 2, R).swapaxes(2, 3).reshape(levels, own, B, R)
    inverse = lax.dynamic_slice_in_dim(diagonal_block_inverse, first, own, 1)
    inverse = inverse.reshape(levels, own, B, B // 2, 2).swapaxes(3, 4).reshape(levels, own, B, B)
    dma = pltpu.SemaphoreType.DMA
    rows = own * PACK
    solved = pl.pallas_call(
        functools.partial(kernel, (levels, sn_dev, slots, Z, Y, X)),
        out_shape=jax.ShapeDtypeStruct((levels, sn_dev, B, R), jnp.bfloat16),
        in_specs=[
            pl.BlockSpec(memory_space=pltpu.SMEM),
            pl.BlockSpec(memory_space=pltpu.VMEM),
            pl.BlockSpec(memory_space=pltpu.VMEM),
            pl.BlockSpec(memory_space=pl.ANY),
        ],
        out_specs=pl.BlockSpec(memory_space=pltpu.VMEM),
        scratch_shapes=[
            pltpu.VMEM((levels - 1, sn_dev, slots, B * B), jnp.bfloat16),
            pltpu.VMEM((levels - 1, sn_dev, B, slots * B), jnp.bfloat16),
            pltpu.VMEM((slots, B // 2, LANES), jnp.float32),
            pltpu.VMEM(((levels - 1) * sn_lev + 1, B, LANES), jnp.bfloat16),
            pltpu.VMEM((col_count, rows, LANES), jnp.float32),
            pltpu.VMEM((levels, rows, LANES), jnp.bfloat16),
            [pltpu.VMEM((col_count, rows, LANES), jnp.float32) for _ in range(levels - 1)],
            [pltpu.VMEM((Z, Y, X, 2, rows, LANES), jnp.bfloat16) for _ in range(levels - 1)],
            pltpu.VMEM((col_count, rows, LANES), jnp.bfloat16),
            dma((levels,)),
            dma((col_count,)),
            dma((levels - 1, col_count)),
            dma((Z,)),
            dma((Y,)),
            dma((X,)),
            dma((1,)),
            dma((levels - 1, Z)),
            dma((levels - 1, Y)),
            dma((levels - 1, X)),
            dma((levels - 1, 2)),
            dma((col_count,)),
            dma((col_count,)),
        ],
        compiler_params=pltpu.CompilerParams(
            collective_id=0, has_side_effects=True, vmem_limit_bytes=60 * 1024 * 1024
        ),
    )(pattern, right, inverse, factor)
    return solved.reshape(levels, sn_dev, B * R)


def solution(mesh):
    return jax.shard_map(
        per_device,
        mesh=mesh,
        in_specs=(
            P(None, "row", None),
            P(None, "row", "col", None),
            P(None, "row", None),
            P(None, "row", "col"),
        ),
        out_specs=P(None, "row", None),
        check_vma=False,
    )
```

time: 354 us -> 83.3 us (0.24)
  blocking collectives: 140 us -> 0 us
  local copies, waits for them, and re-layouts: 89 us -> 9.17 us
  waiting for transfers between devices: 76.1 us -> 0 us
  Pallas kernels: 0 us -> 73.9 us
  matrix products: 19.5 us -> 0 us
  other arithmetic: 14.4 us -> 0 us
  between operations: 13.3 us -> 0.04 us
    all_gather x4 -> x0, blocking collectives: 140 us -> none  [per_device(): complete = lax.all_gather(solved_rows, 'row', axis=0, tiled=True)]
    psum x3 -> x0, waiting for transfers between devices: 76.1 us -> none  [per_device(): summed_products = lax.psum(partial_value, 'col')]
    pallas_call x0 -> x1, Pallas kernels: none -> 73.9 us  [per_device(): pl.pallas_call(functools.partial(kernel, (levels, sn_dev, slots, Z, Y, X)...]
    another operation x14 -> x0, local copies, waits for them, and re-layouts: 37 us -> none  [the longest x3 20.7 us: per_device(): blocks = factor[level].reshape(sn_dev, slot_count, B, B)]
    reshape x3, local copies, waits for them, and re-layouts: 23.4 us -> 3.7 us  [the longest x1 2.54 us: per_device(): return solved.reshape(levels, sn_dev, B * R)]
    dot_general x7 -> x0, matrix products: 19.5 us -> none  [the longest x3 15.8 us: per_device(): jnp.einsum('skab,skbr->sar', blocks, picked, preferred_element_type=jnp.f...]
    gather x3 -> x0, local copies, waits for them, and re-layouts: 12.3 us -> none  [per_device(): jnp.take(panel_blocks, clipped, axis=0).reshape(sn_dev, slot_count, B * R)]
    select_n x6 -> x0, other arithmetic: 11.8 us -> none  [per_device(): jnp.take(panel_blocks, clipped, axis=0).reshape(sn_dev, slot_count, B * R)]
  transfers between devices with their start and end apart: 3 -> 0, of which waited for: 3 -> 0; matrix products, arithmetic and copies ran while one was open for 6% -> 0% of each run, Pallas kernels for 0% -> 0%
where the time goes in v1:
time: 83.3 us; the launch traced here: 83.1 us
  Pallas kernels  73.9 us (89%)
  local copies, waits for them, and re-layouts  9.17 us (11%)
    pallas_call x1, Pallas kernels, per_device(): pl.pallas_call(functools.partial(kernel, (levels, sn_dev, slots, Z, Y, X)...  73.9 us
    reshape x1, local copies, waits for them, and re-layouts, per_device(): return solved.reshape(levels, sn_dev, B * R)  2.54 us
    transpose x1, local copies, waits for them, and re-layouts, per_device(): inverse.reshape(levels, own, B, B // 2, 2).swapaxes(3, 4)  2.5 us
    dynamic_slice x2, local copies, waits for them, and re-layouts, per_device(): inverse = lax.dynamic_slice_in_dim(diagonal_block_inverse, first, own, 1)  2.17 us

profile of v1, /device:TPU:0, one launch (start us, length us, event | category | flops | bytes accessed | tf_op | source)
XLA Modules:
  0.0 83.1 jit_solution(13205447285341660216)
XLA Ops:
  0.0 0.0 copy-start
  0.0 1.1 %constant_dynamic-slice_fusion = bf16[4,2,4096]{2,1,0:T(2,128)(2,1)S(1)} fusion(bf16[4,8,4096]{2,1,0:T(8,128)(2,1)} %param.6, s32[]{:T(128)S(6)} %select_n.4), kind=kLoop, calls=%fused_computation | loop fusion | bytes 131076 | tf_op jit(solution)/shard_map/dynamic_slice | solution.py:279
  1.1 1.1 %copy.6 = bf16[4,2,4096]{0,2,1:T(8,128)(2,1)S(1)} copy(bf16[4,2,4096]{2,1,0:T(2,128)(2,1)S(1)} %constant_dynamic-slice_fusion) | data formatting | bytes 131072 | tf_op jit(solution)/shard_map/dynamic_slice | solution.py:279
  2.2 2.5 %copy.7 = bf16[4,2,64,2,32]{2,4,3,1,0:T(8,128)(2,1)S(1)} copy(bf16[4,2,64,2,32]{0,3,4,2,1:T(2,128)(2,1)S(1)} %bitcast.8) | data formatting | bytes 131072 | tf_op jit(solution)/shard_map/transpose | solution.py:280
  4.7 0.8 copy.8.inverse_ref
  5.5 0.0 copy-done
  5.5 0.1 constant_dynamic-slice_fusion.1
  5.5 0.4 reshape.15
  5.9 0.7 copy.5
  6.7 73.9 %shard_map.46 = bf16[4,8,64,96]{3,2,1,0:T(8,128)(2,1)} custom-call(s32[4,8,32]{2,1,0:T(8,128)} %pattern_ref.1, f32[4,2,64,96]{3,2,1,0:T(8,128)} %bitcast.9, bf16[4,2,64,64]{3,2,1,0:T(8,128)(2,1)} %copy.8.inverse_ref, bf16[4,8,32,4096]{3,2,1,0:T(8,128)(2,1)} %factor_ref.1), custom_call_target="tpu_custom_call" | custom-call | tf_op jit(solution)/shard_map/pallas_call | solution.py:283
  80.5 2.5 %reshape.19 = bf16[4,8,6144]{2,1,0:T(8,128)(2,1)} reshape(bf16[4,8,64,96]{3,2,1,0:T(8,128)(2,1)} %shard_map.46) | data formatting | bytes 786432 | tf_op jit(solution)/shard_map/reshape | solution.py:321
Async XLA Ops:
  0.0 5.5 %copy-start = (f32[4,8,6144]{2,1,0:T(8,128)S(1)}, f32[4,8,6144]{2,1,0:T(8,128)}, u32[]{:S(2)}) copy-start(f32[4,8,6144]{2,1,0:T(8,128)} %param.4) | copy-start | bytes 2359300

commit v2 on v0

v2 whole, which is shorter than its diff:
```python
import functools

import jax
import jax.numpy as jnp
from jax import lax
from jax.experimental import pallas as pl
from jax.experimental.pallas import tpu as pltpu
from jax.sharding import PartitionSpec as P

B = 64
R = 96
LANES = 128
PACK = 48
MESH = pl.DeviceIdType.MESH


def pack(value):
    tail = value[PACK:, :R]
    third = B - PACK
    side = jnp.concatenate([tail[:, 32 * j : 32 * j + 32] for j in range(PACK // third)], axis=0)
    return jnp.concatenate([value[:PACK, :R], side], axis=1)


def unpack_tail(packed):
    third = B - PACK
    parts = [packed[third * j : third * (j + 1), R:] for j in range(PACK // third)]
    return jnp.concatenate(parts, axis=1)


def kernel(
    sizes, pattern_ref, right_ref, inverse_ref, factor_ref, out_ref,
    raw, ready, turn, panels, psend, keep, mine, precv, land, last,
    fsem, red_send, red_recv, z_send, s_send, c_send,
    z_recv, s_recv, c_recv, l_send, l_recv,
):
    levels, sn_dev, slots, Z, A = sizes
    col_count = 2 * A
    row_count = Z * A
    own = sn_dev // col_count
    sn_lev = sn_dev * row_count
    empty = (levels - 1) * sn_lev
    row = lax.axis_index("row")
    col = lax.axis_index("col")
    z, y = row // A, row % A
    x, core = col // 2, col % 2

    def load(level):
        return pltpu.make_async_copy(factor_ref.at[level], raw.at[level - 1], fsem.at[level - 1])

    for level in range(1, levels):
        load(level).start()

    turns = 1 + (z // (Z // 2)) * (Z - 2)
    cols = [(col + d) % col_count for d in range(1, col_count)]

    def plane(d):
        return (z + turns * d) % Z

    def at(r, c):
        return {"row": r, "col": c}

    barrier = pltpu.get_barrier_semaphore()
    for d in range(1, Z):
        pl.semaphore_signal(barrier, inc=1, device_id=at(plane(d) * A + y, col), device_id_type=MESH)
    plane_peers = [
        ((y + d // A) % A, (x + d % A) % A) for d in range(1, A * A)
    ]
    for yt, xt in plane_peers:
        pl.semaphore_signal(barrier, inc=1, device_id=at(z * A + yt, xt * 2 + core), device_id_type=MESH)
    for t in range(A):
        pl.semaphore_signal(barrier, inc=1, device_id=at(row, t * 2 + 1 - core), device_id_type=MESH)

    def remote(src, dst, send, recv, device):
        return pltpu.make_async_remote_copy(
            src_ref=src, dst_ref=dst, send_sem=send, recv_sem=recv,
            device_id=device, device_id_type=MESH,
        )

    def solve(level, summed):
        for u in range(own):
            value = right_ref[level, u]
            if summed is not None:
                value = value - summed[u]
            solved = jnp.dot(
                inverse_ref[level, u], value.astype(jnp.bfloat16), preferred_element_type=jnp.float32
            )
            mine[u * PACK : (u + 1) * PACK, :] = pack(solved).astype(jnp.bfloat16)

    def prepare(level, begin, count):
        low = lax.broadcasted_iota(jnp.int32, (B // 2, LANES), 1) < B

        def body(i, carry):
            for a in range(B // 2):
                turn[:, a, :] = raw[level - 1, i, :, a * LANES : (a + 1) * LANES].astype(jnp.float32)
            for q in range(slots // 2):
                even, odd = turn[2 * q], turn[2 * q + 1]
                lanes = slice(q * LANES, (q + 1) * LANES)
                ready[i, : B // 2, lanes] = jnp.where(low, even, pltpu.roll(odd, B, 1)).astype(jnp.bfloat16)
                ready[i, B // 2 :, lanes] = jnp.where(low, pltpu.roll(even, B, 1), odd).astype(jnp.bfloat16)
            return carry

        lax.fori_loop(begin, begin + count, body, 0)

    def products(level):
        def product(i):
            total = jnp.zeros((B, LANES), jnp.float32)
            for q in range(slots // 4):
                picked = []
                for k in range(4 * q, 4 * q + 4):
                    source = pattern_ref[level, i, k]
                    picked.append(panels[jnp.where(source < 0, empty, source)])
                total += jnp.dot(
                    ready[i, :, 4 * B * q : 4 * B * (q + 1)],
                    jnp.concatenate(picked, axis=0),
                    preferred_element_type=jnp.float32,
                )
            return pack(total)

        def copy(t, source):
            return remote(
                psend.at[t], precv.at[level - 1, source],
                red_send.at[t], red_recv.at[level - 1, source], at(row, t),
            )

        for t in cols:
            def outward(u, carry):
                psend[t, pl.ds(pl.multiple_of(u * PACK, PACK), PACK), :] = product(t * own + u).astype(
                    jnp.bfloat16
                )
                return carry

            lax.fori_loop(0, own, outward, 0)
            copy(t, col).start()

        def inward(u, carry):
            keep[pl.ds(pl.multiple_of(u * PACK, PACK), PACK), :] = product(col * own + u)
            return carry

        lax.fori_loop(0, own, inward, 0)
        summed = keep[...]
        for t in cols:
            copy(t, t).wait_recv()
            summed += precv[level - 1, t].astype(jnp.float32)
        for t in cols:
            copy(t, col).wait_send()
        values = []
        for u in range(own):
            packed = summed[u * PACK : (u + 1) * PACK]
            values.append(jnp.concatenate([packed[:, :R], unpack_tail(packed)], axis=0))
        return values

    def unpack(level, zc, yc, xc, c):
        base = level * sn_lev + (((zc * A + yc) * A + xc) * 2 + c) * own
        for u in range(own):
            packed = land[level, zc, yc, xc, c, u * PACK : (u + 1) * PACK, :]
            panels[base + u, :PACK, :] = packed
            panels[base + u, PACK:, :R] = unpack_tail(packed)

    def gather(level):
        def z_copy(t, source):
            part = land.at[level, source, y, x, core]
            return remote(part, part, z_send.at[t], z_recv.at[level, source], at(t * A + y, col))

        def p_copy(zc, yt, xt, yc, xc):
            part = land.at[level, zc, yc, xc, core]
            return remote(
                part, part, s_send.at[zc, yt, xt], s_recv.at[level, zc, yc, xc],
                at(z * A + yt, xt * 2 + core),
            )

        def c_copy(zc, yc, xc, c):
            part = land.at[level, zc, yc, xc, c]
            return remote(
                part, part, c_send.at[zc, yc, xc], c_recv.at[level, zc, yc, xc],
                at(row, x * 2 + 1 - core),
            )

        def done(zc, yc, xc):
            c_copy(zc, yc, xc, core).start()
            unpack(level, zc, yc, xc, core)

        def chunk(zc):
            for yt, xt in plane_peers:
                p_copy(zc, yt, xt, y, x).start()
            done(zc, y, x)

        def tail(zc):
            for yt, xt in plane_peers:
                p_copy(zc, yt, xt, yt, xt).wait_recv()
                done(zc, yt, xt)

        land[level, z, y, x, core] = mine[...]
        for d in range(1, Z):
            z_copy(plane(d), z).start()
        chunk(z)
        load(level + 1).wait()
        share = sn_dev // Z
        prepare(level + 1, 0, share)

        def body(d, carry):
            zc = plane(d)
            z_copy(zc, zc).wait_recv()
            chunk(zc)
            prepare(level + 1, d * share, share)
            tail(plane(d - 1))
            return carry

        lax.fori_loop(1, Z, body, 0)
        tail(plane(Z - 1))

        def finish(zc, carry):
            for yc in range(A):
                for xc in range(A):
                    c_copy(zc, yc, xc, 1 - core).wait_recv()
                    unpack(level, zc, yc, xc, 1 - core)
            return carry

        lax.fori_loop(0, Z, finish, 0)

        for d in range(1, Z):
            z_copy(plane(d), z).wait_send()

        def settle(zc, carry):
            for yt, xt in plane_peers:
                p_copy(zc, yt, xt, y, x).wait_send()
            for yc in range(A):
                for xc in range(A):
                    c_copy(zc, yc, xc, core).wait_send()
            return carry

        lax.fori_loop(0, Z, settle, 0)

    panels[empty] = jnp.zeros((B, LANES), jnp.bfloat16)
    solve(0, None)
    pl.semaphore_wait(barrier, Z - 1 + A * A - 1 + A)

    def step(level, carry):
        gather(level)
        solve(level + 1, products(level + 1))
        return carry

    lax.fori_loop(0, levels - 1, step, 0)

    top = levels - 1

    def top_copy(t, source):
        return remote(mine, last.at[source], l_send.at[t], l_recv.at[source], at(row, t))

    for t in cols:
        top_copy(t, col).start()
    for level in range(top):
        for i in range(sn_dev):
            out_ref[level, i] = panels[level * sn_lev + row * sn_dev + i, :, :R]
    last[col] = mine[...]
    for t in cols:
        top_copy(t, t).wait_recv()
    for t in cols:
        top_copy(t, col).wait_send()
    for c in range(col_count):
        for u in range(own):
            packed = last[c, u * PACK : (u + 1) * PACK, :]
            out_ref[top, c * own + u, :PACK, :] = packed[:, :R]
            out_ref[top, c * own + u, PACK:, :] = unpack_tail(packed)


def per_device(right_side, factor, diagonal_block_inverse, pattern):
    levels, sn_dev, _ = right_side.shape
    slots = factor.shape[2]
    row_count = lax.axis_size("row")
    col_count = lax.axis_size("col")
    A = col_count // 2
    Z = row_count // A
    own = sn_dev // col_count
    sn_lev = sn_dev * row_count
    first = lax.axis_index("col") * own
    right = lax.dynamic_slice_in_dim(right_side, first, own, 1)
    right = right.reshape(levels, own, B // 2, 2, R).swapaxes(2, 3).reshape(levels, own, B, R)
    inverse = lax.dynamic_slice_in_dim(diagonal_block_inverse, first, own, 1)
    inverse = inverse.reshape(levels, own, B, B // 2, 2).swapaxes(3, 4).reshape(levels, own, B, B)
    dma = pltpu.SemaphoreType.DMA
    rows = own * PACK
    solved = pl.pallas_call(
        functools.partial(kernel, (levels, sn_dev, slots, Z, A)),
        out_shape=jax.ShapeDtypeStruct((levels, sn_dev, B, R), jnp.bfloat16),
        in_specs=[
            pl.BlockSpec(memory_space=pltpu.SMEM),
            pl.BlockSpec(memory_space=pltpu.VMEM),
            pl.BlockSpec(memory_space=pltpu.VMEM),
            pl.BlockSpec(memory_space=pl.ANY),
        ],
        out_specs=pl.BlockSpec(memory_space=pltpu.VMEM),
        scratch_shapes=[
            pltpu.VMEM((levels - 1, sn_dev, slots, B * B), jnp.bfloat16),
            pltpu.VMEM((sn_dev, B, slots * B), jnp.bfloat16),
            pltpu.VMEM((slots, B // 2, LANES), jnp.float32),
            pltpu.VMEM(((levels - 1) * sn_lev + 1, B, LANES), jnp.bfloat16),
            pltpu.VMEM((col_count, rows, LANES), jnp.bfloat16),
            pltpu.VMEM((rows, LANES), jnp.float32),
            pltpu.VMEM((rows, LANES), jnp.bfloat16),
            pltpu.VMEM((levels - 1, col_count, rows, LANES), jnp.bfloat16),
            pltpu.VMEM((levels - 1, Z, A, A, 2, rows, LANES), jnp.bfloat16),
            pltpu.VMEM((col_count, rows, LANES), jnp.bfloat16),
            dma((levels - 1,)),
            dma((col_count,)),
            dma((levels - 1, col_count)),
            dma((Z,)),
            dma((Z, A, A)),
            dma((Z, A, A)),
            dma((levels - 1, Z)),
            dma((levels - 1, Z, A, A)),
            dma((levels - 1, Z, A, A)),
            dma((col_count,)),
            dma((col_count,)),
        ],
        compiler_params=pltpu.CompilerParams(
            collective_id=0, has_side_effects=True, vmem_limit_bytes=60 * 1024 * 1024
        ),
    )(pattern, right, inverse, factor)
    return solved.reshape(levels, sn_dev, B * R)


def solution(mesh):
    return jax.shard_map(
        per_device,
        mesh=mesh,
        in_specs=(
            P(None, "row", None),
            P(None, "row", "col", None),
            P(None, "row", None),
            P(None, "row", "col"),
        ),
        out_specs=P(None, "row", None),
        check_vma=False,
    )
```

time: 354 us -> 71.5 us (0.20)
  blocking collectives: 140 us -> 0 us
  local copies, waits for them, and re-layouts: 89 us -> 9.17 us
  waiting for transfers between devices: 76.1 us -> 0 us
  Pallas kernels: 0 us -> 62 us
  matrix products: 19.5 us -> 0 us
  other arithmetic: 14.4 us -> 0 us
  between operations: 13.3 us -> 0.04 us
    all_gather x4 -> x0, blocking collectives: 140 us -> none  [per_device(): complete = lax.all_gather(solved_rows, 'row', axis=0, tiled=True)]
    psum x3 -> x0, waiting for transfers between devices: 76.1 us -> none  [per_device(): summed_products = lax.psum(partial_value, 'col')]
    pallas_call x0 -> x1, Pallas kernels: none -> 62 us  [per_device(): pl.pallas_call(functools.partial(kernel, (levels, sn_dev, slots, Z, A)),...]
    another operation x14 -> x0, local copies, waits for them, and re-layouts: 37 us -> none  [the longest x3 20.7 us: per_device(): blocks = factor[level].reshape(sn_dev, slot_count, B, B)]
    reshape x3, local copies, waits for them, and re-layouts: 23.4 us -> 3.7 us  [the longest x1 2.54 us: per_device(): return solved.reshape(levels, sn_dev, B * R)]
    dot_general x7 -> x0, matrix products: 19.5 us -> none  [the longest x3 15.8 us: per_device(): jnp.einsum('skab,skbr->sar', blocks, picked, preferred_element_type=jnp.f...]
    gather x3 -> x0, local copies, waits for them, and re-layouts: 12.3 us -> none  [per_device(): jnp.take(panel_blocks, clipped, axis=0).reshape(sn_dev, slot_count, B * R)]
    select_n x6 -> x0, other arithmetic: 11.8 us -> none  [per_device(): jnp.take(panel_blocks, clipped, axis=0).reshape(sn_dev, slot_count, B * R)]
  transfers between devices with their start and end apart: 3 -> 0, of which waited for: 3 -> 0; matrix products, arithmetic and copies ran while one was open for 6% -> 0% of each run, Pallas kernels for 0% -> 0%
where the time goes in v2:
time: 71.5 us; the launch traced here: 71.2 us
  Pallas kernels  62 us (87%)
  local copies, waits for them, and re-layouts  9.17 us (13%)
    pallas_call x1, Pallas kernels, per_device(): pl.pallas_call(functools.partial(kernel, (levels, sn_dev, slots, Z, A)),...  62 us
    reshape x1, local copies, waits for them, and re-layouts, per_device(): return solved.reshape(levels, sn_dev, B * R)  2.54 us
    transpose x1, local copies, waits for them, and re-layouts, per_device(): inverse.reshape(levels, own, B, B // 2, 2).swapaxes(3, 4)  2.5 us
    dynamic_slice x2, local copies, waits for them, and re-layouts, per_device(): inverse = lax.dynamic_slice_in_dim(diagonal_block_inverse, first, own, 1)  2.17 us

profile of v2, /device:TPU:0, one launch (start us, length us, event | category | flops | bytes accessed | tf_op | source)
XLA Modules:
  0.0 71.2 jit_solution(5179035137043018382)
XLA Ops:
  0.0 0.0 copy-start
  0.0 1.1 %constant_dynamic-slice_fusion = bf16[4,2,4096]{2,1,0:T(2,128)(2,1)S(1)} fusion(bf16[4,8,4096]{2,1,0:T(8,128)(2,1)} %param.6, s32[]{:T(128)S(6)} %select_n.4), kind=kLoop, calls=%fused_computation | loop fusion | bytes 131076 | tf_op jit(solution)/shard_map/dynamic_slice | solution.py:278
  1.1 1.1 %copy.6 = bf16[4,2,4096]{0,2,1:T(8,128)(2,1)S(1)} copy(bf16[4,2,4096]{2,1,0:T(2,128)(2,1)S(1)} %constant_dynamic-slice_fusion) | data formatting | bytes 131072 | tf_op jit(solution)/shard_map/dynamic_slice | solution.py:278
  2.2 2.5 %copy.7 = bf16[4,2,64,2,32]{2,4,3,1,0:T(8,128)(2,1)S(1)} copy(bf16[4,2,64,2,32]{0,3,4,2,1:T(2,128)(2,1)S(1)} %bitcast.8) | data formatting | bytes 131072 | tf_op jit(solution)/shard_map/transpose | solution.py:279
  4.7 0.8 %copy.8.inverse_ref = bf16[4,2,64,64]{3,2,1,0:T(8,128)(2,1)} copy(bf16[4,2,64,64]{2,3,1,0:T(8,128)(2,1)S(1)} %bitcast.11) | data formatting | bytes 131072 | tf_op jit(solution)/shard_map/reshape | solution.py:279
  5.5 0.0 copy-done
  5.5 0.1 constant_dynamic-slice_fusion.1
  5.5 0.4 reshape.15
  5.9 0.7 %copy.5 = f32[4,2,2,32,96]{4,3,2,1,0:T(8,128)} copy(f32[4,2,2,32,96]{4,2,3,1,0:T(2,128)S(1)} %bitcast.10) | data formatting | bytes 393216 | tf_op jit(solution)/shard_map/transpose | solution.py:277
  6.7 62.0 %shard_map.46 = bf16[4,8,64,96]{3,2,1,0:T(8,128)(2,1)} custom-call(s32[4,8,32]{2,1,0:T(8,128)} %pattern_ref.1, f32[4,2,64,96]{3,2,1,0:T(8,128)} %bitcast.9, bf16[4,2,64,64]{3,2,1,0:T(8,128)(2,1)} %copy.8.inverse_ref, bf16[4,8,32,4096]{3,2,1,0:T(8,128)(2,1)} %factor_ref.1), custom_call_target="tpu_custom_call" | custom-call | tf_op jit(solution)/shard_map/pallas_call | solution.py:282
  68.7 2.5 %reshape.19 = bf16[4,8,6144]{2,1,0:T(8,128)(2,1)} reshape(bf16[4,8,64,96]{3,2,1,0:T(8,128)(2,1)} %shard_map.46) | data formatting | bytes 786432 | tf_op jit(solution)/shard_map/reshape | solution.py:319
Async XLA Ops:
  0.0 5.5 %copy-start = (f32[4,8,6144]{2,1,0:T(8,128)S(1)}, f32[4,8,6144]{2,1,0:T(8,128)}, u32[]{:S(2)}) copy-start(f32[4,8,6144]{2,1,0:T(8,128)} %param.4) | copy-start | bytes 2359300

commit v3 on v2

--- a/solution.py
+++ b/solution.py
@@ -29,7 +29,7 @@
 
 def kernel(
     sizes, pattern_ref, right_ref, inverse_ref, factor_ref, out_ref,
-    raw, ready, turn, panels, psend, keep, mine, precv, land, last,
+    raw, ready, turn, panels, psend, keep, wide, mine, precv, land, last,
     fsem, red_send, red_recv, z_send, s_send, c_send,
     z_recv, s_recv, c_recv, l_send, l_recv,
 ):
@@ -101,7 +101,7 @@
 
         lax.fori_loop(begin, begin + count, body, 0)
 
-    def products(level):
+    def products(level, sent):
         def product(i):
             total = jnp.zeros((B, LANES), jnp.float32)
             for q in range(slots // 4):
@@ -124,9 +124,7 @@
 
         for t in cols:
             def outward(u, carry):
-                psend[t, pl.ds(pl.multiple_of(u * PACK, PACK), PACK), :] = product(t * own + u).astype(
-                    jnp.bfloat16
-                )
+                psend[t, pl.ds(pl.multiple_of(u * PACK, PACK), PACK), :] = product(t * own + u)
                 return carry
 
             lax.fori_loop(0, own, outward, 0)
@@ -137,16 +135,21 @@
             return carry
 
         lax.fori_loop(0, own, inward, 0)
+        sent()
         summed = keep[...]
         for t in cols:
             copy(t, t).wait_recv()
-            summed += precv[level - 1, t].astype(jnp.float32)
+            summed += precv[level - 1, t]
         for t in cols:
             copy(t, col).wait_send()
         values = []
         for u in range(own):
             packed = summed[u * PACK : (u + 1) * PACK]
-            values.append(jnp.concatenate([packed[:, :R], unpack_tail(packed)], axis=0))
+            split = jnp.concatenate([packed[:, :R], unpack_tail(packed)], axis=0)
+            split = jnp.concatenate([split, jnp.zeros((B, LANES - R), jnp.float32)], axis=1)
+            for p in range(2):
+                wide[u, pl.ds(p, B // 2, stride=2), :] = split[p * (B // 2) : (p + 1) * (B // 2)]
+            values.append(wide[u, :, :R])
         return values
 
     def unpack(level, zc, yc, xc, c):
@@ -217,9 +220,6 @@
 
         lax.fori_loop(0, Z, finish, 0)
 
-        for d in range(1, Z):
-            z_copy(plane(d), z).wait_send()
-
         def settle(zc, carry):
             for yt, xt in plane_peers:
                 p_copy(zc, yt, xt, y, x).wait_send()
@@ -228,15 +228,20 @@
                     c_copy(zc, yc, xc, core).wait_send()
             return carry
 
-        lax.fori_loop(0, Z, settle, 0)
+        def sent():
+            for d in range(1, Z):
+                z_copy(plane(d), z).wait_send()
+            lax.fori_loop(0, Z, settle, 0)
+
+        return sent
 
     panels[empty] = jnp.zeros((B, LANES), jnp.bfloat16)
     solve(0, None)
     pl.semaphore_wait(barrier, Z - 1 + A * A - 1 + A)
 
     def step(level, carry):
-        gather(level)
-        solve(level + 1, products(level + 1))
+        sent = gather(level)
+        solve(level + 1, products(level + 1, sent))
         return carry
 
     lax.fori_loop(0, levels - 1, step, 0)
@@ -274,9 +279,9 @@
     sn_lev = sn_dev * row_count
     first = lax.axis_index("col") * own
     right = lax.dynamic_slice_in_dim(right_side, first, own, 1)
-    right = right.reshape(levels, own, B // 2, 2, R).swapaxes(2, 3).reshape(levels, own, B, R)
+    right = right.reshape(levels, own, B, R)
     inverse = lax.dynamic_slice_in_dim(diagonal_block_inverse, first, own, 1)
-    inverse = inverse.reshape(levels, own, B, B // 2, 2).swapaxes(3, 4).reshape(levels, own, B, B)
+    inverse = inverse.reshape(levels, own, B, B)
     dma = pltpu.SemaphoreType.DMA
     rows = own * PACK
     solved = pl.pallas_call(
@@ -294,10 +299,11 @@
             pltpu.VMEM((sn_dev, B, slots * B), jnp.bfloat16),
             pltpu.VMEM((slots, B // 2, LANES), jnp.float32),
             pltpu.VMEM(((levels - 1) * sn_lev + 1, B, LANES), jnp.bfloat16),
-            pltpu.VMEM((col_count, rows, LANES), jnp.bfloat16),
+            pltpu.VMEM((col_count, rows, LANES), jnp.float32),
             pltpu.VMEM((rows, LANES), jnp.float32),
+            pltpu.VMEM((own, B, LANES), jnp.float32),
             pltpu.VMEM((rows, LANES), jnp.bfloat16),
-            pltpu.VMEM((levels - 1, col_count, rows, LANES), jnp.bfloat16),
+            pltpu.VMEM((levels - 1, col_count, rows, LANES), jnp.float32),
             pltpu.VMEM((levels - 1, Z, A, A, 2, rows, LANES), jnp.bfloat16),
             pltpu.VMEM((col_count, rows, LANES), jnp.bfloat16),
             dma((levels - 1,)),

time: 71.5 us -> 67.9 us (0.950); the launches traced: 71.2 us -> 66.9 us
  local copies, waits for them, and re-layouts: 9.17 us -> 5.42 us
    transpose x2 -> x0, local copies, waits for them, and re-layouts: 3.23 us -> none  [the longest x1 2.5 us: per_device(): inverse.reshape(levels, own, B, B // 2, 2).swapaxes(3, 4)]
    dynamic_slice x2 -> x1, local copies, waits for them, and re-layouts: 2.17 us -> 1.09 us  [per_device(): inverse = lax.dynamic_slice_in_dim(diagonal_block_inverse, first, own, 1)]
where the time goes in v3:
time: 67.9 us; the launch traced here: 66.9 us
  Pallas kernels  61.4 us (90%)
  local copies, waits for them, and re-layouts  5.42 us (8%)
    pallas_call x1, Pallas kernels, per_device(): pl.pallas_call(functools.partial(kernel, (levels, sn_dev, slots, Z, A)),...  61.4 us
    reshape x1, local copies, waits for them, and re-layouts, per_device(): return solved.reshape(levels, sn_dev, B * R)  2.54 us

profile of v3, /device:TPU:0, one launch (start us, length us, event | category | flops | bytes accessed | tf_op | source)
XLA Modules:
  0.0 66.9 jit_solution(7925286951165092167)
XLA Ops:
  0.0 0.0 copy-start
  0.0 1.1 %constant_dynamic-slice_fusion = bf16[4,2,4096]{2,1,0:T(2,128)(2,1)S(1)} fusion(bf16[4,8,4096]{2,1,0:T(8,128)(2,1)} %param.6, s32[]{:T(128)S(6)} %select_n.4), kind=kLoop, calls=%fused_computation | loop fusion | bytes 131076 | tf_op jit(solution)/shard_map/dynamic_slice | solution.py:283
  1.1 0.8 %reshape.10.inverse_ref = bf16[4,2,64,64]{3,2,1,0:T(8,128)(2,1)} reshape(bf16[4,2,4096]{2,1,0:T(2,128)(2,1)S(1)} %constant_dynamic-slice_fusion) | data formatting | bytes 131072 | tf_op jit(solution)/shard_map/reshape | solution.py:284
  1.9 0.0 copy-done
  1.9 0.1 constant_dynamic-slice_fusion.1
  2.0 0.9 %reshape.9.right_ref = f32[4,2,64,96]{3,2,1,0:T(8,128)} reshape(f32[4,2,6144]{2,1,0:T(2,128)S(1)} %constant_dynamic-slice_fusion.1) | data formatting | bytes 393216 | tf_op jit(solution)/shard_map/reshape | solution.py:282
  2.9 61.4 %shard_map.46 = bf16[4,8,64,96]{3,2,1,0:T(8,128)(2,1)} custom-call(s32[4,8,32]{2,1,0:T(8,128)} %pattern_ref.1, f32[4,2,64,96]{3,2,1,0:T(8,128)} %reshape.9.right_ref, bf16[4,2,64,64]{3,2,1,0:T(8,128)(2,1)} %reshape.10.inverse_ref, bf16[4,8,32,4096]{3,2,1,0:T(8,128)(2,1)} %factor_ref.1), custom_call_target="tpu_custom_call" | custom-call | tf_op jit(solution)/shard_map/pallas_call | solution.py:287
  64.3 2.5 %reshape.11 = bf16[4,8,6144]{2,1,0:T(8,128)(2,1)} reshape(bf16[4,8,64,96]{3,2,1,0:T(8,128)(2,1)} %shard_map.46) | data formatting | bytes 786432 | tf_op jit(solution)/shard_map/reshape | solution.py:325
Async XLA Ops:
  0.0 1.9 %copy-start = (f32[4,8,6144]{2,1,0:T(8,128)S(1)}, f32[4,8,6144]{2,1,0:T(8,128)}, u32[]{:S(2)}) copy-start(f32[4,8,6144]{2,1,0:T(8,128)} %param.4) | copy-start | bytes 2359300
